TPU v7x, 512 devices: a whole 4x4x16 slice. The times are simulated.
512 devices in a mesh: fsdp: 64 (over y, z_hi, x, core), basis: 8 (over z_lo).
Axes of the slice: x: 4, y: 4, z: 16 (z_hi: 2, z_lo: 8; z = z_hi * 8 + z_lo), core: 2. Of those that a mesh axis runs over, the one named last changes fastest.
Arguments:
- activations: bfloat16 [2048, 6144], P('basis', 'fsdp'), may hold values from -6 to 6
- hidden_grad: bfloat16 [2048, 8192], P('basis', 'fsdp'), may hold values from -0.1796875 to 0.1796875
- block_rows: int32 [16], P('basis'), may hold values from 1 to 128, 1280 in all
- basis: bfloat16 [6144, 4096], P('fsdp', 'basis'), may hold values from -0.21875 to 0.21875
- accumulated: float32 [6144, 8192], P('basis', 'fsdp'), may hold values from -3 to 3
Outputs:
- projected: float32 [6144, 8192], P('basis', 'fsdp')
Inputs may be any that keep to these rules, and one draw needn't show every extreme that they name: `block_rows`: every block holds at least one routed token, and some block is full.
All inputs are finite; a program needn't handle non-finite values.
Results may differ from a plain program's by a relative error of at most 0.029.
Values may be sent and summed in bfloat16 or wider, within the bound.
No kernel may reach another device: no remote copies, remote signals or barrier semaphores. Data moves between devices by JAX's collectives and lax.ppermute only.
A program may use at most 64 MiB of HBM per device.

v0:
```python
import jax
import jax.numpy as jnp
from jax import lax
from jax.sharding import PartitionSpec as P

BLOCK = 128


def on_device(activations, hidden_grad, block_rows, basis, accumulated):
    block_size = BLOCK
    tok_count = activations.shape[0]
    blocks_here = block_rows.shape[0]
    position = jnp.arange(tok_count, dtype=jnp.int32)
    block_index = position // block_size
    fill_count = jnp.sum(
        jnp.where(
            block_index[:, None] == jnp.arange(blocks_here, dtype=jnp.int32)[None, :],
            block_rows[None, :],
            0,
        ),
        axis=1,
    )
    live_rows = position % block_size < fill_count
    masked = jnp.where(live_rows[:, None], hidden_grad, jnp.zeros_like(hidden_grad))
    features = lax.all_gather(activations, "fsdp", axis=1, tiled=True)
    partial_value = lax.dot_general(
        features, masked, (((0,), (0,)), ((), ())), preferred_element_type=jnp.float32
    )
    row_count = partial_value.shape[0] // lax.axis_size("basis")
    row_start = lax.axis_index("basis") * row_count
    current = lax.dynamic_slice_in_dim(partial_value, row_start, row_count, 0)
    partial_value = lax.dynamic_update_slice_in_dim(
        partial_value, current + accumulated, row_start, 0
    )
    gradient = lax.psum(partial_value.astype(jnp.bfloat16), "basis")
    own_rows = lax.dynamic_slice_in_dim(gradient, row_start, row_count, 0)
    panel_full = lax.all_gather(basis, "fsdp", axis=0, tiled=True)
    coeff_sum = lax.dot_general(
        panel_full, gradient, (((0,), (0,)), ((), ())), preferred_element_type=jnp.float32
    )
    coeffs = coeff_sum.astype(jnp.bfloat16)
    removal_part = jnp.dot(panel_full, coeffs, preferred_element_type=jnp.float32)
    removed = lax.psum_scatter(
        removal_part.astype(jnp.bfloat16), "basis", scatter_dimension=0, tiled=True
    ).astype(jnp.float32)
    return own_rows.astype(jnp.float32) - removed


def solution(mesh):
    placed = (
        P("basis", "fsdp"),
        P("basis", "fsdp"),
        P("basis"),
        P("fsdp", "basis"),
        P("basis", "fsdp"),
    )
    return jax.shard_map(
        on_device, mesh=mesh, in_specs=placed, out_specs=P("basis", "fsdp"), check_vma=False
    )
```

profile of v0, /device:TPU:12, one launch (start us, length us, event | category | flops | bytes accessed | tf_op | source)
XLA Modules:
  0.0 496.8 jit_solution(16144019380713073946)
XLA Ops:
  6.5 0.0 all-gather.3.cloned.1.call-start
  6.5 0.7 all-gather.3.cloned.1.call-update
  7.3 0.0 all-reduce.2.cloned.1.call-start
  7.3 1.2 copy.8
  8.5 0.7 fusion.6
  9.2 127.1 %all-gather.3.cloned.1.call-done = bf16[256,6144]{0,1:T(8,128)(2,1)} async-done(((bf16[256,96]{0,1:T(8,128)(2,1)}), bf16[256,6144]{0,1:T(8,128)(2,1)}) %all-gather.3.cloned.1.call-update) | async-done | bytes 3145744 | tf_op jit(solution)/shard_map/all_gather | solution.py:25
  136.4 3.2 fusion.2
  139.6 0.3 copy.10
  139.9 0.1 fusion.1
  139.9 1.4 convert_element_type.19
  141.3 0.0 all-reduce.2.cloned.1.call-update
  141.4 0.0 all-gather.5.cloned.1.call-start
  141.4 0.7 all-gather.5.cloned.1.call-update
  142.1 0.0 reduce-scatter.2.cloned.1.call-start
  142.1 124.4 %all-reduce.2.cloned.1.call-done = bf16[6144,128]{0,1:T(8,128)(2,1)} async-done(((bf16[6144,128]{0,1:T(8,128)(2,1)}), bf16[6144,128]{0,1:T(8,128)(2,1)}) %all-reduce.2.cloned.1.call-update) | async-done | bytes 1572880 | tf_op jit(solution)/shard_map/psum | solution.py:35
  266.5 146.4 %all-gather.5.cloned.1.call-done = bf16[6144,512]{1,0:T(8,128)(2,1)} async-done(((bf16[96,512]{1,0:T(8,128)(2,1)}), bf16[6144,512]{1,0:T(8,128)(2,1)}) %all-gather.5.cloned.1.call-update) | async-done | bytes 6291472 | tf_op jit(solution)/shard_map/all_gather | solution.py:37
  412.9 9.3 %fusion = bf16[6144,128]{0,1:T(8,128)(2,1)} fusion(bf16[6144,512]{1,0:T(8,128)(2,1)} %all-gather.5.cloned.1.call-done, bf16[6144,128]{0,1:T(8,128)(2,1)} %all-reduce.2.cloned.1.call-done), kind=kOutput, calls=%fused_computation.1 | convolution fusion | flops 1611464704 | bytes 9437184 | tf_op jit(solution)/shard_map/dot_general | solution.py:42
  422.3 0.0 reduce-scatter.2.cloned.1.call-update
  422.3 66.0 %reduce-scatter.2.cloned.1.call-done = bf16[768,128]{0,1:T(8,128)(2,1)} async-done(((bf16[6144,128]{0,1:T(8,128)(2,1)}), bf16[768,128]{0,1:T(8,128)(2,1)}) %reduce-scatter.2.cloned.1.call-update) | async-done | bytes 196624 | tf_op jit(solution)/shard_map/reduce_scatter | solution.py:43
  488.3 1.1 convert_subtract_fusion
  489.3 0.9 copy.9
  (2 shorter events, 0.0 us)
Async XLA Ops:
  6.5 129.8 %all-gather.3.cloned.1.call-start = ((), (), s32[]{:S(2)}) async-start(), calls=%async_computation.1 | async-start | bytes 3194880 | tf_op jit(solution)/shard_map/all_gather | solution.py:25
  7.3 259.3 %all-reduce.2.cloned.1.call-start = ((), (), s32[]{:S(2)}) async-start(), calls=%async_computation.2 | async-start | bytes 3145728 | tf_op jit(solution)/shard_map/psum | solution.py:35
  141.4 271.6 %all-gather.5.cloned.1.call-start = ((), (), s32[]{:S(2)}) async-start(), calls=%async_computation.3 | async-start | bytes 6389760 | tf_op jit(solution)/shard_map/all_gather | solution.py:37
  142.1 346.2 %reduce-scatter.2.cloned.1.call-start = ((), (), s32[]{:S(2)}) async-start(), calls=%async_computation.4 | async-start | bytes 1769472 | tf_op jit(solution)/shard_map/reduce_scatter | solution.py:43
Sparse Core Ops, SparseCore 0:
  11.9 124.4 all-gather.2
  141.5 124.9 all-reduce.1
  271.0 141.8 all-gather.4
  422.4 65.8 reduce-scatter.1
where the time goes:
time: 497 us
  waiting for transfers between devices  465 us (94%)
  between operations  13.2 us (3%)
  matrix products  12.5 us (3%)
    all_gather x1, waiting for transfers between devices, on_device(): panel_full = lax.all_gather(basis, 'fsdp', axis=0, tiled=True)  146 us
    all_gather x1, waiting for transfers between devices, on_device(): features = lax.all_gather(activations, 'fsdp', axis=1, tiled=True)  127 us
    psum x1, waiting for transfers between devices, on_device(): gradient = lax.psum(partial_value.astype(jnp.bfloat16), 'basis')  124 us
    reduce_scatter x1, waiting for transfers between devices, on_device(): lax.psum_scatter(removal_part.astype(jnp.bfloat16), 'basis', scatter_dime...  66 us
  transfers between devices with their start and end apart: 4, of which 4 were waited for; matrix products, arithmetic and copies ran while one was open for 0% of the time, Pallas kernels for 0%

commit v1 on v0

--- a/solution.py
+++ b/solution.py
@@ -34,7 +34,9 @@
     )
     gradient = lax.psum(partial_value.astype(jnp.bfloat16), "basis")
     own_rows = lax.dynamic_slice_in_dim(gradient, row_start, row_count, 0)
-    panel_full = lax.all_gather(basis, "fsdp", axis=0, tiled=True)
+    panel_full = jnp.concatenate(
+        lax.all_to_all(jnp.stack([basis] * lax.axis_size("fsdp")), "fsdp", 0, 0), axis=0
+    )
     coeff_sum = lax.dot_general(
         panel_full, gradient, (((0,), (0,)), ((), ())), preferred_element_type=jnp.float32
     )

time: 497 us -> 597 us (1.20)
  the two profiles are of different devices: /device:TPU:12 before, /device:TPU:4 now
where the time goes in v1:
time: 597 us
  waiting for transfers between devices  542 us (91%)
  starting transfers between devices  21.7 us (4%)
  between operations  13.2 us (2%)
  matrix products  12.4 us (2%)
    all_gather x1, waiting for transfers between devices, on_device(): features = lax.all_gather(activations, 'fsdp', axis=1, tiled=True)  351 us
    psum x1, waiting for transfers between devices, on_device(): gradient = lax.psum(partial_value.astype(jnp.bfloat16), 'basis')  124 us
    reduce_scatter x1, waiting for transfers between devices, on_device(): lax.psum_scatter(removal_part.astype(jnp.bfloat16), 'basis', scatter_dime...  65.9 us
    all_to_all x1, starting transfers between devices, on_device(): lax.all_to_all(jnp.stack([basis] * lax.axis_size('fsdp')), 'fsdp', 0, 0)  21.5 us
  transfers between devices with their start and end apart: 4, of which 3 were waited for; matrix products, arithmetic and copies ran while one was open for 1% of the time, Pallas kernels for 0%

profile of v1, /device:TPU:4, one launch (start us, length us, event | category | flops | bytes accessed | tf_op | source)
XLA Modules:
  0.0 597.2 jit_solution(13193170596614928737)
XLA Ops:
  6.5 4.3 stack.2
  10.8 0.0 copy-start
  10.8 0.0 copy-start.2
  10.8 0.0 copy-start.1
  10.8 21.5 %all-to-all-start = ((bf16[64,96,512]{2,1,0:T(8,128)(2,1)}), bf16[64,96,512]{2,1,0:T(8,128)(2,1)}, u32[]{:S(2)}, u32[]{:S(2)}) async-start(bf16[64,96,512]{2,1,0:T(8,128)(2,1)} %stack.2), calls=%async_computation | async-start | bytes 12582912 | tf_op jit(solution)/shard_map/all_to_all | solution.py:38
  32.4 0.0 all-gather.2.cloned.1.call-start
  32.4 0.7 all-gather.2.cloned.1.call-update
  33.1 0.0 all-reduce.2.cloned.1.call-start
  33.2 0.0 copy-done
  33.2 0.2 copy.8
  33.4 0.0 copy-done.2
  33.4 0.1 fusion.6
  33.5 350.9 %all-gather.2.cloned.1.call-done = bf16[256,6144]{0,1:T(8,128)(2,1)} async-done(((bf16[256,96]{0,1:T(8,128)(2,1)}), bf16[256,6144]{0,1:T(8,128)(2,1)}) %all-gather.2.cloned.1.call-update) | async-done | bytes 3145744 | tf_op jit(solution)/shard_map/all_gather | solution.py:25
  384.4 0.0 copy-done.1
  384.4 3.1 fusion.2
  387.5 0.3 copy.10
  387.8 0.1 fusion.1
  387.9 1.3 convert_element_type.19
  389.2 0.0 all-reduce.2.cloned.1.call-update
  389.2 0.0 reduce-scatter.2.cloned.1.call-start
  389.3 124.2 %all-reduce.2.cloned.1.call-done = bf16[6144,128]{0,1:T(8,128)(2,1)} async-done(((bf16[6144,128]{0,1:T(8,128)(2,1)}), bf16[6144,128]{0,1:T(8,128)(2,1)}) %all-reduce.2.cloned.1.call-update) | async-done | bytes 1572880 | tf_op jit(solution)/shard_map/psum | solution.py:35
  513.5 0.0 all-to-all-done
  513.5 9.3 %fusion = bf16[6144,128]{0,1:T(8,128)(2,1)} fusion(bf16[6144,512]{1,0:T(8,128)(2,1)} %bitcast.2, bf16[6144,128]{0,1:T(8,128)(2,1)} %all-reduce.2.cloned.1.call-done), kind=kOutput, calls=%fused_computation.1 | convolution fusion | flops 1611464704 | bytes 9437184 | tf_op jit(solution)/shard_map/dot_general | solution.py:44
  522.7 0.0 reduce-scatter.2.cloned.1.call-update
  522.8 65.9 %reduce-scatter.2.cloned.1.call-done = bf16[768,128]{0,1:T(8,128)(2,1)} async-done(((bf16[6144,128]{0,1:T(8,128)(2,1)}), bf16[768,128]{0,1:T(8,128)(2,1)}) %reduce-scatter.2.cloned.1.call-update) | async-done | bytes 196624 | tf_op jit(solution)/shard_map/reduce_scatter | solution.py:45
  588.7 1.1 convert_subtract_fusion
  589.7 0.9 copy.9
  (2 shorter events, 0.0 us)
Async XLA Ops:
  10.8 22.3 %copy-start = (f32[768,128]{1,0:T(8,128)S(1)}, f32[768,128]{1,0:T(8,128)}, u32[]{:S(2)}) copy-start(f32[768,128]{1,0:T(8,128)} %param.9) | copy-start | bytes 1179652
  10.8 22.5 %copy-start.2 = (s32[2]{0:T(128)S(1)}, s32[2]{0:T(128)}, u32[]{:S(2)}) copy-start(s32[2]{0:T(128)} %param.7) | copy-start | bytes 28
  10.8 373.5 %copy-start.1 = (bf16[256,128]{1,0:T(8,128)(2,1)S(1)}, bf16[256,128]{1,0:T(8,128)(2,1)}, u32[]{:S(2)}) copy-start(bf16[256,128]{1,0:T(8,128)(2,1)} %param.6) | copy-start | bytes 196612
  10.8 502.6 %all-to-all-start = ((bf16[64,96,512]{2,1,0:T(8,128)(2,1)}), bf16[64,96,512]{2,1,0:T(8,128)(2,1)}, u32[]{:S(2)}, u32[]{:S(2)}) async-start(bf16[64,96,512]{2,1,0:T(8,128)(2,1)} %stack.2), calls=%async_computation | async-start | bytes 12582912 | tf_op jit(solution)/shard_map/all_to_all | solution.py:38
  32.4 352.0 %all-gather.2.cloned.1.call-start = ((), (), s32[]{:S(2)}) async-start(), calls=%async_computation.2 | async-start | bytes 3194880 | tf_op jit(solution)/shard_map/all_gather | solution.py:25
  33.1 480.4 %all-reduce.2.cloned.1.call-start = ((), (), s32[]{:S(2)}) async-start(), calls=%async_computation.3 | async-start | bytes 3145728 | tf_op jit(solution)/shard_map/psum | solution.py:35
  389.2 199.4 %reduce-scatter.2.cloned.1.call-start = ((), (), s32[]{:S(2)}) async-start(), calls=%async_computation.4 | async-start | bytes 1769472 | tf_op jit(solution)/shard_map/reduce_scatter | solution.py:45
Sparse Core Ops, SparseCore 0:
  37.7 346.5 all-gather.1
  389.4 124.0 all-reduce.1
  522.9 65.7 reduce-scatter.1

commit v2 on v0

--- a/solution.py
+++ b/solution.py
@@ -32,7 +32,7 @@
     partial_value = lax.dynamic_update_slice_in_dim(
         partial_value, current + accumulated, row_start, 0
     )
-    gradient = lax.psum(partial_value.astype(jnp.bfloat16), "basis")
+    gradient = jnp.sum(lax.all_gather(partial_value.astype(jnp.bfloat16), "basis"), axis=0)
     own_rows = lax.dynamic_slice_in_dim(gradient, row_start, row_count, 0)
     panel_full = lax.all_gather(basis, "fsdp", axis=0, tiled=True)
     coeff_sum = lax.dot_general(

time: 497 us -> 624 us (1.26)
  the two profiles are of different devices: /device:TPU:12 before, /device:TPU:4 now
where the time goes in v2:
time: 624 us
  waiting for transfers between devices  572 us (92%)
  local copies, waits for them, and re-layouts  14.1 us (2%)
  between operations  13.2 us (2%)
  other arithmetic  12.2 us (2%)
  matrix products  12.1 us (2%)
    all_gather x1, waiting for transfers between devices, on_device(): lax.all_gather(partial_value.astype(jnp.bfloat16), 'basis')  249 us
    all_gather x1, waiting for transfers between devices, on_device(): panel_full = lax.all_gather(basis, 'fsdp', axis=0, tiled=True)  130 us
    all_gather x1, waiting for transfers between devices, on_device(): features = lax.all_gather(activations, 'fsdp', axis=1, tiled=True)  128 us
    reduce_scatter x1, waiting for transfers between devices, on_device(): lax.psum_scatter(removal_part.astype(jnp.bfloat16), 'basis', scatter_dime...  63.9 us
    unnamed x3, local copies, waits for them, and re-layouts  13.2 us
  transfers between devices with their start and end apart: 4, of which 4 were waited for; matrix products, arithmetic and copies ran while one was open for 4% of the time, Pallas kernels for 0%

profile of v2, /device:TPU:4, one launch (start us, length us, event | category | flops | bytes accessed | tf_op | source)
XLA Modules:
  0.0 623.5 jit_solution(16785186358180661422)
XLA Ops:
  6.5 0.0 all-gather.5.cloned.1.call-start
  6.5 0.7 all-gather.5.cloned.1.call-update
  7.3 0.0 all-gather.9.cloned.1.call-start
  7.3 1.2 copy.8
  8.5 0.7 fusion.6
  9.2 127.9 %all-gather.5.cloned.1.call-done = bf16[256,6144]{0,1:T(8,128)(2,1)} async-done(((bf16[256,96]{0,1:T(8,128)(2,1)}), bf16[256,6144]{0,1:T(8,128)(2,1)}) %all-gather.5.cloned.1.call-update) | async-done | bytes 3145744 | tf_op jit(solution)/shard_map/all_gather | solution.py:25
  137.1 3.2 fusion.2
  140.3 0.3 copy.11
  140.6 0.1 fusion.1
  140.6 1.3 convert_element_type.21
  142.0 0.0 all-gather.9.cloned.1.call-update
  142.0 0.0 all-gather.7.cloned.1.call-start
  142.1 0.7 all-gather.7.cloned.1.call-update
  142.7 0.0 reduce-scatter.2.cloned.1.call-start
  142.8 249.0 %all-gather.9.cloned.1.call-done = bf16[49152,128]{0,1:T(8,128)(2,1)} async-done(((bf16[6144,128]{0,1:T(8,128)(2,1)}), bf16[49152,128]{0,1:T(8,128)(2,1)}) %all-gather.9.cloned.1.call-update) | async-done | bytes 12582928 | tf_op jit(solution)/shard_map/all_gather | solution.py:35
  391.8 11.7 %copy.10 = bf16[16,8,8,6144]{3,2,1,0:T(8,128)(2,1)S(1)} copy(bf16[16,8,8,6144]{3,1,2,0:T(8,128)(2,1)} %bitcast.17) | data formatting | bytes 25165824
  403.6 9.1 %bitcast_reduce_fusion = bf16[6144,128]{0,1:T(8,128)(2,1)S(1)} fusion(bf16[16,8,8,6144]{3,2,1,0:T(8,128)(2,1)S(1)} %copy.10), kind=kLoop, calls=%fused_computation | loop fusion | flops 5505024 | bytes 14155776 | tf_op jit(solution)/shard_map/reduce_sum | solution.py:35
  412.7 129.6 %all-gather.7.cloned.1.call-done = bf16[6144,512]{1,0:T(8,128)(2,1)} async-done(((bf16[96,512]{1,0:T(8,128)(2,1)}), bf16[6144,512]{1,0:T(8,128)(2,1)}) %all-gather.7.cloned.1.call-update) | async-done | bytes 6291472 | tf_op jit(solution)/shard_map/all_gather | solution.py:37
  542.2 8.9 %fusion = bf16[6144,128]{0,1:T(8,128)(2,1)} fusion(bf16[6144,512]{1,0:T(8,128)(2,1)} %all-gather.7.cloned.1.call-done, bf16[6144,128]{0,1:T(8,128)(2,1)S(1)} %bitcast_reduce_fusion), kind=kOutput, calls=%fused_computation.2 | convolution fusion | flops 1611464704 | bytes 9437184 | tf_op jit(solution)/shard_map/dot_general | solution.py:42
  551.1 0.0 reduce-scatter.2.cloned.1.call-update
  551.2 63.9 %reduce-scatter.2.cloned.1.call-done = bf16[768,128]{0,1:T(8,128)(2,1)} async-done(((bf16[6144,128]{0,1:T(8,128)(2,1)}), bf16[768,128]{0,1:T(8,128)(2,1)}) %reduce-scatter.2.cloned.1.call-update) | async-done | bytes 196624 | tf_op jit(solution)/shard_map/reduce_scatter | solution.py:43
  615.1 1.0 convert_subtract_fusion
  616.1 0.9 copy.9
  (2 shorter events, 0.0 us)
Async XLA Ops:
  6.5 130.6 %all-gather.5.cloned.1.call-start = ((), (), s32[]{:S(2)}) async-start(), calls=%async_computation.1 | async-start | bytes 3194880 | tf_op jit(solution)/shard_map/all_gather | solution.py:25
  7.3 384.6 %all-gather.9.cloned.1.call-start = ((), (), s32[]{:S(2)}) async-start(), calls=%async_computation.4 | async-start | bytes 14155776 | tf_op jit(solution)/shard_map/all_gather | solution.py:35
  142.0 400.2 %all-gather.7.cloned.1.call-start = ((), (), s32[]{:S(2)}) async-start(), calls=%async_computation.2 | async-start | bytes 6389760 | tf_op jit(solution)/shard_map/all_gather | solution.py:37
  142.7 472.3 %reduce-scatter.2.cloned.1.call-start = ((), (), s32[]{:S(2)}) async-start(), calls=%async_computation.3 | async-start | bytes 1769472 | tf_op jit(solution)/shard_map/reduce_scatter | solution.py:43
Sparse Core Ops, SparseCore 0:
  11.9 125.1 all-gather.4
  142.1 249.6 all-gather.8
  396.4 145.8 all-gather.6
  551.3 63.7 reduce-scatter.1
